TPU v7x, 1024 devices: a whole 4x8x16 slice. The times are simulated.
1024 devices in a mesh: user: 8 (over y), item: 128 (over x, z, core).
Axes of the slice: x: 4, y: 8, z: 16, core: 2. Of those that a mesh axis runs over, the one named last changes fastest.
Arguments:
- features: bfloat16 [262144, 2048], P(('user', 'item')), may hold values from -6 to 6
- w_out: bfloat16 [2048, 256], replicated, may hold values from -0.125 to 0.125
- interests: bfloat16 [65536, 8, 256], P(('user', 'item')), may hold values from -136 to 136
- neg_tiles: int32 [65536, 4], P(('user', 'item')), may hold values from 0 to 15
- positives: int32 [65536], P(('user', 'item')), may hold values from 0 to 2047
- tile_valid: int32 [2048], P(('user', 'item')), may hold values from 1 to 128
Outputs:
- grad_w: float32 [2048, 256], P('item')
- grad_interests: float32 [65536, 8, 256], P(('user', 'item'))
- user_loss: float32 [65536], P(('user', 'item'))
Inputs may be any that keep to these rules, and one draw needn't show every extreme that they name: `neg_tiles`: tile numbers within the user's group. `positives`: item numbers within the user's group. `tile_valid`: live slots are the first ones of a tile.
All inputs are finite; a program needn't handle non-finite values.
Results may differ from a plain program's by a relative error of at most 0.012.
The roundings to bfloat16 on the way count: a program that leaves them out, or rounds other values in their place, can miss the bound.
Values may be sent and summed in bfloat16 or wider, within the bound.
A program may use at most 32 MiB of HBM per device.

v0:
```python
import jax
import jax.numpy as jnp
from jax import lax
from jax.sharding import PartitionSpec as P


def local(features, w_out, interests, neg_tiles, positives, tile_valid):
    embedded = jnp.dot(features, w_out, preferred_element_type=jnp.float32).astype(jnp.bfloat16)
    catalogue, gathered_counts = (
        lax.all_gather(embedded, "user", axis=0, tiled=True),
        lax.all_gather(tile_valid.astype(jnp.bfloat16), "user", axis=0, tiled=True),
    )
    counts = gathered_counts.astype(jnp.int32)
    user_count, interest_count, feature_width = interests.shape
    item_count = catalogue.shape[0]
    tile_count = counts.shape[0]
    tile_size = item_count // tile_count
    queries = interests.reshape(user_count * interest_count, feature_width)
    scores = lax.dot_general(
        queries, catalogue, (((1,), (1,)), ((), ())), preferred_element_type=jnp.float32
    )
    scores = (scores * feature_width ** (-0.5)).reshape(user_count, interest_count, item_count)
    tile_hits = jnp.sum(
        (neg_tiles[:, :, None] == jnp.arange(tile_count, dtype=jnp.int32)[None, None, :]).astype(
            jnp.float32
        ),
        axis=1,
    )
    live_mask = (jnp.arange(tile_size, dtype=jnp.int32)[None, :] < counts[:, None]).astype(
        jnp.float32
    )
    weight = (tile_hits[:, :, None] * live_mask[None]).reshape(user_count, 1, item_count)
    onehot = (
        (jnp.arange(item_count, dtype=jnp.int32)[None, :] == positives[:, None])
        .astype(jnp.float32)
        .reshape(user_count, 1, item_count)
    )
    pos_score = jnp.sum(onehot * scores, axis=-1)
    chosen = weight > 0
    highest = jnp.maximum(pos_score, jnp.max(jnp.where(chosen, scores, -jnp.inf), axis=-1))
    exp_terms = weight * jnp.exp(jnp.where(chosen, scores - highest[..., None], 0.0))
    pos_term = jnp.exp(pos_score - highest)
    denominator = pos_term + jnp.sum(exp_terms, axis=-1)
    user_loss = jnp.sum(highest + jnp.log(denominator) - pos_score, axis=-1)
    score_grad = (
        exp_terms / denominator[..., None] + onehot * (pos_term / denominator - 1.0)[..., None]
    ).astype(jnp.bfloat16)
    flat_grad = score_grad.reshape(user_count * interest_count, item_count)
    query_grads = jnp.dot(flat_grad, catalogue, preferred_element_type=jnp.float32).reshape(
        user_count, interest_count, feature_width
    )
    item_part = lax.dot_general(
        flat_grad, queries, (((0,), (0,)), ((), ())), preferred_element_type=jnp.float32
    ).astype(jnp.bfloat16)
    owner_grad = (
        lax.psum_scatter(item_part, "user", scatter_dimension=0, tiled=True)
        .astype(jnp.float32)
        .astype(jnp.bfloat16)
    )
    weight_part = lax.dot_general(
        features, owner_grad, (((0,), (0,)), ((), ())), preferred_element_type=jnp.float32
    )
    rows_part = lax.psum_scatter(weight_part, "item", scatter_dimension=0, tiled=True)
    grad_w = lax.psum(rows_part, "user")
    return (grad_w, query_grads, user_loss)


def solution(mesh):
    in_specs = (
        P(("user", "item"), None),
        P(),
        P(("user", "item"), None, None),
        P(("user", "item"), None),
        P(("user", "item")),
        P(("user", "item")),
    )
    out_specs = (P("item", None), P(("user", "item"), None, None), P(("user", "item")))
    return jax.shard_map(local, mesh=mesh, in_specs=in_specs, out_specs=out_specs, check_vma=False)
```

profile of v0, /device:TPU:6, one launch (start us, length us, event | category | flops | bytes accessed | tf_op | source)
XLA Modules:
  0.0 440.5 jit_solution(6196601246235580214)
XLA Ops:
  7.2 1.2 copy-done
  8.4 2.3 convolution_convert_fusion
  10.8 0.7 convert_element_type.38
  11.5 1.3 dynamic-slice
  13.4 0.2 dynamic-update-slice
  13.6 17.6 %all-reduce = bf16[16]{0:T(256)(128)(2,1)S(1)} all-reduce(bf16[16]{0:T(256)(128)(2,1)S(1)} %dynamic-update-slice), channel_id=1, replica_groups=mesh['user'=8,'item'=128] {'user'}, use_global_device_ids=true, to_apply=%add | all-reduce | flops 16 | bytes 64
  31.3 0.7 convert_reduce_fusion
  32.0 0.1 copy.15
  32.1 0.2 mul.73
  32.3 0.9 broadcast_compare_fusion
  33.3 32.0 %all-gather.2.cloned.1.call-done = bf16[2048,256]{1,0:T(8,128)(2,1)} async-done(((bf16[256,256]{1,0:T(8,128)(2,1)}), bf16[2048,256]{1,0:T(8,128)(2,1)}) %all-gather.2.cloned.1.call-update) | async-done | bytes 1048592 | tf_op jit(solution)/shard_map/all_gather | solution.py:10
  65.2 4.5 %fusion = (f32[512]{0:T(512)S(1)}, f32[512]{0:T(512)S(1)}, f32[2048,512]{0,1:T(8,128)}) fusion(pred[64,2048]{1,0:T(8,128)(4,1)S(1)} %get-tuple-element.19, f32[64,2048]{1,0:T(8,128)S(1)} %get-tuple-element.26, bf16[2048,256]{1,0:T(8,128)(2,1)} %all-gather.2.cloned.1.call-done, bf16[64,8,256]{2,1,0:T(8,128)(2,1)S(1)} %copy-done.3), kind=kOutput, calls=%fused_computation.4 | convolution fusion | flops 542112768 | bytes 6164480 | tf_op jit(solution)/shard_map/dot_general | solution.py:19
  69.9 3.2 fusion.12
  73.1 0.1 reduce_sum.44
  73.2 0.6 subtract_reduce_fusion
  73.9 5.5 %fusion.13 = bf16[2048,256]{1,0:T(8,128)(2,1)} fusion(bf16[64,8,256]{2,1,0:T(8,128)(2,1)S(1)} %copy-done.3, f32[2048,512]{0,1:T(8,128)} %get-tuple-element.25, f32[64,8]{1,0:T(8,128)S(1)} %get-tuple-element.22, f32[64,8]{1,0:T(8,128)S(1)} %get-tuple-element.21, f32[64,8]{1,0:T(8,128)S(1)} %get-tuple-element.18, f32[64,2048]{1,0:T(8,128)S(1)} %get-tuple-element.26, ...), kind=kOutput, calls=%fused_computation.21 | convolution fusion | flops 545783808 | bytes 6690816 | tf_op jit(solution)/shard_map/dot_general | solution.py:52
  79.5 45.6 %reduce-scatter.5.cloned.1.call-done = bf16[256,256]{1,0:T(8,128)(2,1)} async-done(((bf16[2048,256]{1,0:T(8,128)(2,1)}), bf16[256,256]{1,0:T(8,128)(2,1)}) %reduce-scatter.5.cloned.1.call-update) | async-done | bytes 131088 | tf_op jit(solution)/shard_map/reduce_scatter | solution.py:56
  125.0 1.4 convolution_bitcast_fusion
  126.4 1.9 copy.17
  128.3 5.4 %fusion.14 = f32[64,8,256]{2,1,0:T(8,128)} fusion(f32[2048,512]{0,1:T(8,128)} %get-tuple-element.25, f32[512]{0:T(512)S(1)} %get-tuple-element.24, f32[512]{0:T(512)S(1)} %get-tuple-element.23, f32[512]{0:T(512)S(1)} %max.19, f32[64,2048]{1,0:T(8,128)} %copy-done.2, f32[64,2048]{1,0:T(8,128)} %copy-done.1, pred[64,2048]{1,0:T(8,128)(4,1)S(1)} %get-tuple-element.19, ...), kind=kOutput, calls=%fused_computation.22 | convolution fusion | flops 545259520 | bytes 6952960 | tf_op jit(solution)/shard_map/dot_general | solution.py:49
  133.6 267.6 %reduce-scatter.7.cloned.1.call-done = f32[16,256]{1,0:T(8,128)} async-done(((f32[2048,256]{1,0:T(8,128)}), f32[16,256]{1,0:T(8,128)}) %reduce-scatter.7.cloned.1.call-update) | async-done | bytes 16400
  401.3 0.8 copy.18
  402.1 31.2 %psum.7 = f32[16,256]{0,1:T(8,128)S(1)} all-reduce(f32[16,256]{0,1:T(8,128)S(1)} %copy.18), channel_id=1, replica_groups=mesh['user'=8,'item'=128] {'user'}, use_global_device_ids=true, to_apply=%region_6.7 | all-reduce | flops 4096 | bytes 32768 | tf_op jit(solution)/shard_map/psum | solution.py:64
  433.3 0.7 copy.16
  (22 shorter events, 0.5 us)
Async XLA Ops:
  7.2 1.2 copy-start
  7.2 58.0 %copy-start.3 = (bf16[64,8,256]{2,1,0:T(8,128)(2,1)S(1)}, bf16[64,8,256]{2,1,0:T(8,128)(2,1)}, u32[]{:S(2)}) copy-start(bf16[64,8,256]{2,1,0:T(8,128)(2,1)} %param.8) | copy-start | bytes 786436
  7.2 58.0 %all-gather.2.cloned.1.call-start = ((), (), s32[]{:S(2)}) async-start(), calls=%async_computation.2 | async-start | bytes 1179648 | tf_op jit(solution)/shard_map/all_gather | solution.py:10
  10.7 114.3 %reduce-scatter.5.cloned.1.call-start = ((), (), s32[]{:S(2)}) async-start(), calls=%async_computation.3 | async-start | bytes 1179648 | tf_op jit(solution)/shard_map/reduce_scatter | solution.py:56
  33.2 40.7 %copy-start.1 = (f32[64,2048]{1,0:T(8,128)}, f32[64,2048]{1,0:T(8,128)S(1)}, u32[]{:S(2)}) copy-start(f32[64,2048]{1,0:T(8,128)S(1)} %get-tuple-element.20) | copy-start | bytes 1572868
  33.3 40.7 %copy-start.2 = (f32[64,2048]{1,0:T(8,128)}, f32[64,2048]{1,0:T(8,128)S(1)}, u32[]{:S(2)}) copy-start(f32[64,2048]{1,0:T(8,128)S(1)} %get-tuple-element.26) | copy-start | bytes 1572868
  79.4 321.9 %reduce-scatter.7.cloned.1.call-start = ((), (), s32[]{:S(2)}) async-start(), calls=%async_computation.4 | async-start | bytes 2113536
Sparse Core Ops, SparseCore 0:
  11.3 53.9 all-gather.1
  79.5 45.4 reduce-scatter.4
  130.8 270.4 reduce-scatter.6
where the time goes:
time: 441 us; the launch traced here: 440 us
  waiting for transfers between devices  345 us (78%)
  blocking collectives  48.8 us (11%)
  matrix products  19 us (4%)
  between operations  14.5 us (3%)
  local copies, waits for them, and re-layouts  6.66 us (2%)
  other arithmetic  6.18 us (1%)
    unnamed x4, waiting for transfers between devices  268 us
    reduce_scatter x1, waiting for transfers between devices, local(): lax.psum_scatter(item_part, 'user', scatter_dimension=0, tiled=True)  45.6 us
    all_gather x1, waiting for transfers between devices, local(): lax.all_gather(embedded, 'user', axis=0, tiled=True)  32 us
    psum x1, blocking collectives, local(): grad_w = lax.psum(rows_part, 'user')  31.2 us
    unnamed x1, blocking collectives  17.6 us
  transfers between devices with their start and end apart: 3, of which 3 were waited for; matrix products, arithmetic and copies ran while one was open for 2% of the time, Pallas kernels for 0%

commit v1 on v0

v1 whole, which is shorter than its diff:
```python
import functools
from types import SimpleNamespace

import jax
import jax.numpy as jnp
from jax import lax
from jax.experimental import pallas as pl
from jax.experimental.pallas import tpu as pltpu
from jax.sharding import PartitionSpec as P

MESH = pl.DeviceIdType.MESH
NX, NZ, NC = 4, 16, 2
TILE = 128
DEPTHS = 4
PIECES = 4
ROWS = 32
LOW = -1e30
F32, BF16 = jnp.float32, jnp.bfloat16

NAMES = (
    "features", "w_out", "interests", "negatives", "positives", "valid",
    "grad_w", "grad_interests", "user_loss",
    "feat", "feat_t", "w", "q", "qs", "cat", "cnt", "neg_rows", "expo", "prob", "m_rows", "l_rows", "p_rows",
    "query_grad", "item_part", "item_grad",
    "ring_up", "ring_down", "feat_s", "item_sib", "w_own", "x_two", "x_up", "x_down", "x_own", "xr_two_up",
    "xr_two_down", "xr_up", "xr_down",
    "y_send", "y_own", "y_recv", "z_send", "z_own", "z_recv", "g_buf",
    "local_sem", "cnt_send", "cnt_recv", "gather_send", "gather_recv", "ring_send", "ring_recv", "core_send",
    "core_recv",
    "x_send", "x_recv", "y_ssem", "y_rsem", "z_ssem", "z_rsem", "g_ssem", "g_rsem",
)


def dot(a, b, dims):
    return lax.dot_general(a, b, ((dims[:1], dims[1:]), ((), ())), preferred_element_type=F32)


def kernel(ny, *refs):
    r = SimpleNamespace(**dict(zip(NAMES, refs, strict=True)))
    half = ny // 2
    users, kk = r.positives.shape[1], r.q.shape[0] // r.positives.shape[1]
    lanes = users * kk
    items = r.feat.shape[0]
    y = lax.axis_index("user")
    item = lax.axis_index("item")
    core = lax.rem(item, NC)
    z = lax.rem(item // NC, NZ)
    x = item // (NC * NZ)

    def at(y2, x2, z2, c2):
        return (y2, (x2 * NZ + z2) * NC + c2)

    def y_peer(d):
        return at(lax.rem(y + d + ny, ny), x, z, core)

    def x_peer(d):
        return at(y, lax.rem(x + d + NX, NX), z, core)

    def z_peer(d):
        return at(y, x, lax.rem(z + d, NZ), core)

    sibling = at(y, x, z, 1 - core)
    pending = []

    def send(src, dst, send_sem, recv_sem, device):
        copy = pltpu.make_async_remote_copy(
            src_ref=src, dst_ref=dst, send_sem=send_sem, recv_sem=recv_sem, device_id=device, device_id_type=MESH
        )
        copy.start()
        pending.append(copy)
        return copy

    depth = r.feat.shape[1] // DEPTHS
    parts_w, parts_f = [], []
    for i in range(DEPTHS):
        cut = pl.ds(i * depth, depth)
        parts_w.append(pltpu.make_async_copy(r.w_out.at[cut], r.w.at[cut], r.local_sem.at[2 + 2 * i]))
        parts_f.append(pltpu.make_async_copy(r.features.at[:, cut], r.feat.at[:, cut], r.local_sem.at[3 + 2 * i]))
        parts_w[i].start()
        parts_f[i].start()
    copy_q = pltpu.make_async_copy(r.interests, r.q, r.local_sem.at[0])
    copy_q.start()
    barrier = pltpu.get_barrier_semaphore()

    def greet(device):
        pl.semaphore_signal(barrier, inc=1, device_id=device, device_id_type=MESH)

    for d in range(1, ny):
        greet(y_peer(d))
    greet(sibling)
    greet(x_peer(1))
    greet(x_peer(-1))

    def greet_z(d, carry):
        greet(z_peer(d))
        return carry

    lax.fori_loop(1, NZ, greet_z, 0)

    own_counts = jnp.where(lax.broadcasted_iota(jnp.int32, (8, TILE), 0) == 0, r.valid[0], r.valid[1])
    r.cnt[y] = own_counts
    embedded = jnp.zeros((items, r.w.shape[1]), F32)
    for i in range(DEPTHS):
        parts_w[i].wait()
        parts_f[i].wait()
        cut = slice(i * depth, (i + 1) * depth)
        embedded = embedded + dot(r.feat[:, cut], r.w[cut, :], (1, 0))
    r.cat[0:2] = embedded.astype(BF16).reshape(2, TILE, r.w.shape[1])
    pl.semaphore_wait(barrier, (ny - 1) + 1 + 2 + (NZ - 1))

    gather = {}

    piece = 2 * TILE // PIECES
    per_tile = PIECES // 2

    def pass_on(up, step, part):
        here, there = (step - 1, step) if up else ((ny - step + 1) % ny, ny - step)
        way, slot = (0 if up else 1), PIECES * (step - 1) + part
        rows = pl.ds(part % per_tile * piece, piece)
        tile = part // per_tile
        gather[up, step, part] = send(
            r.cat.at[2 * here + tile, rows],
            r.cat.at[2 * there + tile, rows],
            r.gather_send.at[way, slot],
            r.gather_recv.at[way, slot],
            y_peer(1 if up else -1),
        )

    for part in range(PIECES):
        pass_on(True, 1, part)
        pass_on(False, 1, PIECES - 1 - part)
    counts = [
        send(r.cnt.at[y], r.cnt.at[y], r.cnt_send.at[d], r.cnt_recv.at[d], y_peer(d)) for d in range(1, ny)
    ]

    copy_q.wait()
    r.qs[...] = (r.q[...].astype(F32) * r.q.shape[1] ** -0.5).astype(BF16)
    owner_of_lane = lax.broadcasted_iota(jnp.int32, (users, lanes), 1) // kk
    of_user = owner_of_lane == lax.broadcasted_iota(jnp.int32, (users, lanes), 0)
    diagonal = lax.broadcasted_iota(jnp.int32, (users, users), 0) == lax.broadcasted_iota(
        jnp.int32, (users, users), 1
    )

    def to_lanes(column):
        return jnp.sum(jnp.where(of_user, column, 0.0), axis=0, keepdims=True)

    def to_row(values):
        spread = jnp.broadcast_to(values.astype(F32), (users, users))
        column = jnp.sum(jnp.where(diagonal, spread, 0.0), axis=1, keepdims=True)
        return to_lanes(column).astype(jnp.int32)

    n_neg = r.negatives.shape[0]
    for j in range(n_neg):
        r.neg_rows[j : j + 1, :] = to_row(r.negatives[j : j + 1, :])
    pos_row = to_row(r.positives[...])

    def origin(block):
        return lax.rem(y - block + ny, ny)

    def positive_slot(block, tile):
        first = (origin(block) * 2 + tile) * TILE
        return pos_row - first

    def fold(values, op):
        parts = values.reshape(ROWS // 8, 8, lanes)
        return op(parts, axis=0)

    def row_ids(i):
        return lax.broadcasted_iota(jnp.int32, (ROWS, lanes), 0) + i * ROWS

    counted = {0}

    def score_tile(block, tile):
        if block not in counted:
            counts[block - 1].wait_recv()
            counted.add(block)
        u = origin(block)
        index = 2 * block + tile
        first = tile * TILE
        r.expo[block, first : first + TILE, :] = dot(r.cat[index], r.qs[...], (1, 1))
        number = u * 2 + tile
        hit = jnp.zeros((1, lanes), F32)
        for j in range(n_neg):
            hit = hit + jnp.where(r.neg_rows[j : j + 1, :] == number, 1.0, 0.0)
        live = r.cnt[u][tile : tile + 1, :]
        live = jnp.concatenate([live] * (lanes // TILE), axis=1)
        live = jnp.where(hit > 0, live, 0)
        slot = positive_slot(block, tile)

        def mask(i, carry):
            peak, picked = carry
            rows = pl.ds(first + i * ROWS, ROWS)
            s = r.expo[block, rows, :]
            ids = row_ids(i)
            kept = jnp.where(ids < live, s, LOW)
            r.expo[block, rows, :] = kept
            picked = picked + fold(jnp.where(ids == slot, s, 0.0), jnp.sum)
            return jnp.maximum(peak, fold(kept, jnp.max)), picked

        peak, picked = lax.fori_loop(
            0, TILE // ROWS, mask, (jnp.full((8, lanes), LOW, F32), jnp.zeros((8, lanes), F32))
        )
        m = jnp.max(peak, axis=0, keepdims=True)

        def exponent(i, total):
            rows = pl.ds(first + i * ROWS, ROWS)
            e = hit * jnp.exp(r.expo[block, rows, :] - m)
            r.expo[block, rows, :] = e
            return total + fold(e, jnp.sum)

        total = lax.fori_loop(0, TILE // ROWS, exponent, jnp.zeros((8, lanes), F32))
        r.m_rows[index : index + 1, :] = m
        r.l_rows[index : index + 1, :] = jnp.sum(total, axis=0, keepdims=True)
        r.p_rows[index : index + 1, :] = jnp.sum(picked, axis=0, keepdims=True)

    def transpose_features(x2):
        depth = r.feat.shape[1] // NX
        turned = r.feat[:, x2 * depth : (x2 + 1) * depth].T.reshape(NZ, NC, 16, items)
        for c in range(NC):
            part = turned[:, c].reshape(NZ * 16, items)
            r.feat_t[c, x2 * NZ * 16 : (x2 + 1) * NZ * 16, :] = part

    score_tile(0, 0)
    score_tile(0, 1)
    ready = []
    turns = list(range(NX))
    for step in range(1, half + 1):
        for i in range(PIECES if step < half else per_tile):
            for up, part in ((True, i), (False, PIECES - 1 - i)):
                gather[up, step, part].wait_recv()
                if step + 1 < half or (step + 1 == half and i < per_tile):
                    pass_on(up, step + 1, part)
            if ready:
                score_tile(*ready.pop(0))
            if turns:
                transpose_features(turns.pop(0))
            if i % per_tile == per_tile - 1:
                ready += [(step, i // per_tile), ((ny - step) % ny, 1 - i // per_tile)]
    for x2 in turns:
        transpose_features(x2)
    feat_copy = send(r.feat_t.at[1 - core], r.feat_s, r.core_send.at[2], r.core_recv.at[2], sibling)
    for block, tile in ready:
        score_tile(block, tile)
    m_all = r.m_rows[...]
    pos_score = jnp.sum(r.p_rows[...], axis=0, keepdims=True)
    highest = jnp.maximum(pos_score, jnp.max(m_all, axis=0, keepdims=True))
    factor = jnp.exp(m_all - highest)
    pos_term = jnp.exp(pos_score - highest)
    denominator = pos_term + jnp.sum(factor * r.l_rows[...], axis=0, keepdims=True)
    r.m_rows[...] = factor / denominator
    pos_grad = pos_term / denominator - 1.0

    def grad_block(block):
        for tile in range(2):
            share = r.m_rows[2 * block + tile : 2 * block + tile + 1, :]
            slot = positive_slot(block, tile)

            def normalise(i, carry, tile=tile, slot=slot, share=share):
                first = tile * TILE + i * ROWS
                e = r.expo[block, pl.ds(first, ROWS), :]
                g = e * share + jnp.where(row_ids(i) == slot, pos_grad, 0.0)
                r.prob[pl.ds(block * 2 * TILE + first, ROWS), :] = g.astype(BF16)
                return carry

            lax.fori_loop(0, TILE // ROWS, normalise, 0)
        part = dot(r.prob[block * 2 * TILE : (block + 1) * 2 * TILE, :], r.q[...], (1, 0)).astype(BF16)
        r.item_part[block, 0] = part[:, :TILE]
        r.item_part[block, 1] = part[:, TILE:]

    arms = {}

    def own_block(up, k):
        return (ny - half + k) if up else (half - k)

    part_rows = items // 2

    def landing(up, k, h, v):
        return (r.ring_up if up else r.ring_down).at[2 * k + h, pl.ds(v * part_rows, part_rows)]

    def ring(up, k, h, v):
        way = 0 if up else 1
        slot = 4 * k + 2 * h + v
        arms[up, k, h, v] = send(
            r.item_part.at[own_block(up, k) % ny, h, pl.ds(v * part_rows, part_rows)],
            landing(up, k, h, v),
            r.ring_send.at[way, slot],
            r.ring_recv.at[way, slot],
            y_peer(1 if up else -1),
        )

    def arrived(up, k, h, v):
        arms[up, k, h, v].wait_recv()
        return landing(up, k, h, v)[...].astype(F32)

    def add_and_ring(up, k, h):
        block = own_block(up, k) % ny
        for v in range(2):
            own = r.item_part.at[block, h, pl.ds(v * part_rows, part_rows)]
            own[...] = (own[...].astype(F32) + arrived(up, k - 1, h, v)).astype(BF16)
            ring(up, k, h, v)

    def ring_own(up, k, h):
        for v in range(2):
            ring(up, k, h, v)

    grad_block(half)
    ring_own(True, 0, 0)
    ring_own(False, 0, 1)
    grad_block(own_block(True, 1))
    ring_own(True, 1, 1)
    grad_block(own_block(False, 1))
    ring_own(False, 1, 0)
    grad_block(own_block(True, 2))
    add_and_ring(True, 1, 0)
    add_and_ring(False, 1, 1)
    grad_block(own_block(False, 2))

    def query_part(blocks, first):
        rows = 2 * TILE
        total = None
        for block in blocks:
            c = r.cat[2 * block : 2 * block + 2].reshape(rows, r.q.shape[1])
            part = dot(r.prob[block * rows : (block + 1) * rows, :], c, (0, 0))
            total = part if total is None else total + part
        r.query_grad[...] = total if first else r.query_grad[...] + total

    for k in range(2, half):
        add_and_ring(True, k, 1)
        add_and_ring(False, k, 0)
        if k + 1 < half:
            grad_block(own_block(True, k + 1))
        else:
            query_part(range(half - 2, half + 1), True)
        add_and_ring(True, k, 0)
        add_and_ring(False, k, 1)
        if k + 1 < half:
            grad_block(own_block(False, k + 1))
    grad_block(0)
    copy_g = pltpu.make_async_copy(r.query_grad, r.grad_interests, r.local_sem.at[1])
    others = [b for b in range(ny) if not half - 2 <= b <= half]
    query_part(others[:2], False)

    def finish_queries():
        query_part(others[2:], False)
        copy_g.start()
        loss_row = highest + jnp.log(denominator) - pos_score
        loss_column = jnp.sum(jnp.where(of_user, loss_row, 0.0), axis=1, keepdims=True)
        r.user_loss[...] = jnp.sum(jnp.where(diagonal, loss_column, 0.0), axis=0, keepdims=True)

    block_rows = NZ * 16
    mid = block_rows // 2
    core_copy, x_copy = {}, {}

    def weight_part(h):
        parts = []
        for v in range(2):
            own = r.item_part[0, h, v * part_rows : (v + 1) * part_rows, :].astype(F32)
            parts.append(own + arrived(True, half - 1, h, v) + arrived(False, half - 1, h, v))
        item_grad = jnp.concatenate(parts, axis=0).astype(BF16)
        r.item_grad[h] = item_grad
        core_copy[h] = send(r.item_grad.at[h], r.item_sib.at[h], r.core_send.at[h], r.core_recv.at[h], sibling)

    def x_send(h, kind, src, dst, up):
        x_copy[h, kind] = send(src, dst, r.x_send.at[h, kind], r.x_recv.at[h, kind], x_peer(1 if up else -1))

    def x_first(h):
        r.w_own[h] = dot(r.feat_t[core], r.item_grad[h], (1, 0))
        if h == 0:
            feat_copy.wait_recv()
        core_copy[h].wait_recv()
        r.w_own[h] = r.w_own[h] + dot(r.feat_s[...], r.item_sib[h], (1, 0))

        def block_of(owner):
            rows = pl.ds(pl.multiple_of(lax.rem(owner + NX, NX) * block_rows, block_rows), block_rows)
            return r.w_own[h, rows, :]

        r.x_two[h] = block_of(x + 2).astype(BF16)
        x_send(h, 0, r.x_two.at[h, pl.ds(0, mid)], r.xr_two_up.at[h], True)
        x_send(h, 1, r.x_two.at[h, pl.ds(mid, mid)], r.xr_two_down.at[h], False)
        r.x_up[h] = block_of(x + 1).astype(BF16)
        x_send(h, 2, r.x_up.at[h, pl.ds(mid, mid)], r.xr_up.at[h, pl.ds(mid, mid)], True)
        r.x_down[h] = block_of(x - 1).astype(BF16)
        x_send(h, 3, r.x_down.at[h, pl.ds(0, mid)], r.xr_down.at[h, pl.ds(0, mid)], False)
        r.x_own[h] = block_of(x)

    def x_second(h):
        x_copy[h, 0].wait_recv()
        r.x_up[h, pl.ds(0, mid)] = (r.x_up[h, pl.ds(0, mid)].astype(F32) + r.xr_two_up[h].astype(F32)).astype(BF16)
        x_send(h, 4, r.x_up.at[h, pl.ds(0, mid)], r.xr_up.at[h, pl.ds(0, mid)], True)
        x_copy[h, 1].wait_recv()
        r.x_down[h, pl.ds(mid, mid)] = (
            r.x_down[h, pl.ds(mid, mid)].astype(F32) + r.xr_two_down[h].astype(F32)
        ).astype(BF16)
        x_send(h, 5, r.x_down.at[h, pl.ds(mid, mid)], r.xr_down.at[h, pl.ds(mid, mid)], False)

    per_y = NZ // ny

    def y_stage(h):
        for kind in (2, 3, 4, 5):
            x_copy[h, kind].wait_recv()
        total = (r.x_own[h] + r.xr_up[h].astype(F32) + r.xr_down[h].astype(F32)).reshape(ny, per_y, 16, TILE)
        r.y_own[h] = total
        r.y_send[h] = total.astype(BF16)
        y_copy[h] = [
            send(
                r.y_send.at[h, lax.rem(y + d, ny)], r.y_recv.at[h, d], r.y_ssem.at[h, d], r.y_rsem.at[h, d], y_peer(d)
            )
            for d in range(1, ny)
        ]

    def z_copy(h, i, sender):
        owner = y * per_y + i
        return pltpu.make_async_remote_copy(
            src_ref=r.z_send.at[h, i],
            dst_ref=r.z_recv.at[h, sender],
            send_sem=r.z_ssem.at[h, i],
            recv_sem=r.z_rsem.at[h, sender],
            device_id=at(y, x, owner, core),
            device_id_type=MESH,
        )

    def z_stage(h):
        total = r.y_own[h, y]
        for d, copy in enumerate(y_copy[h], 1):
            copy.wait_recv()
            total = total + r.y_recv[h, d].astype(F32)
        r.z_own[h] = total
        r.z_send[h] = total.astype(BF16)
        for i in range(per_y):

            @pl.when(z != y * per_y + i)
            def _(i=i):
                z_copy(h, i, z).start()

    owns = z // per_y == y

    def g_copy(h, d):
        return pltpu.make_async_remote_copy(
            src_ref=r.g_buf.at[h],
            dst_ref=r.g_buf.at[h],
            send_sem=r.g_ssem.at[h, d],
            recv_sem=r.g_rsem.at[h],
            device_id=y_peer(d),
            device_id_type=MESH,
        )

    def g_stage(h):
        @pl.when(owns)
        def _():
            def add(d, total):
                sender = lax.rem(z + d, NZ)
                z_copy(h, 0, sender).wait_recv()
                return total + r.z_recv[h, sender].astype(F32)

            r.g_buf[h] = lax.fori_loop(1, NZ, add, r.z_own[h, lax.rem(z, per_y)])
            for d in range(1, ny):
                g_copy(h, d).start()

    def finish(h):
        @pl.when(jnp.logical_not(owns))
        def _():
            g_copy(h, 1).wait_recv()

        r.grad_w[:, h * TILE : (h + 1) * TILE] = r.g_buf[h]

    y_copy = {}
    for stage in (weight_part, x_first, x_second, y_stage, z_stage, g_stage, finish):
        for h in range(2):
            stage(h)
        if stage is x_first:
            finish_queries()

    for copy in pending:
        copy.wait_send()

    for h in range(2):
        for i in range(per_y):

            @pl.when(z != y * per_y + i)
            def _(h=h, i=i):
                z_copy(h, i, z).wait_send()

    @pl.when(owns)
    def _():
        for h in range(2):
            for d in range(1, ny):
                g_copy(h, d).wait_send()

    copy_g.wait()


def local(ny, features, w_out, interests, neg_tiles, positives, tile_valid):
    items, depth = features.shape
    width = w_out.shape[1]
    users, kk, _ = interests.shape
    lanes = users * kk
    rows = depth // (NX * NZ * NC)
    half_rows = NX * NZ * rows
    block = NZ * rows
    vmem, dma = pltpu.VMEM, pltpu.SemaphoreType.DMA
    scratch = [
        vmem((items, depth), BF16),
        vmem((NC, half_rows, items), BF16),
        vmem((depth, width), BF16),
        vmem((lanes, width), BF16),
        vmem((lanes, width), BF16),
        vmem((2 * ny, TILE, width), BF16),
        vmem((ny, 8, TILE), jnp.int32),
        vmem((8, lanes), jnp.int32),
        vmem((ny, items, lanes), F32),
        vmem((ny * items, lanes), BF16),
        vmem((2 * ny, lanes), F32),
        vmem((2 * ny, lanes), F32),
        vmem((2 * ny, lanes), F32),
        vmem((lanes, width), F32),
        vmem((ny, 2, items, TILE), BF16),
        vmem((2, items, TILE), BF16),
        vmem((ny, items, TILE), BF16),
        vmem((ny, items, TILE), BF16),
        vmem((half_rows, items), BF16),
        vmem((2, items, TILE), BF16),
        vmem((2, half_rows, TILE), F32),
        vmem((2, block, TILE), BF16),
        vmem((2, block, TILE), BF16),
        vmem((2, block, TILE), BF16),
        vmem((2, block, TILE), F32),
        vmem((2, block // 2, TILE), BF16),
        vmem((2, block // 2, TILE), BF16),
        vmem((2, block, TILE), BF16),
        vmem((2, block, TILE), BF16),
        vmem((2, ny, NZ // ny, rows, TILE), BF16),
        vmem((2, ny, NZ // ny, rows, TILE), F32),
        vmem((2, ny, NZ // ny, rows, TILE), BF16),
        vmem((2, NZ // ny, rows, TILE), BF16),
        vmem((2, NZ // ny, rows, TILE), F32),
        vmem((2, NZ, rows, TILE), BF16),
        vmem((2, rows, TILE), F32),
        dma((2 + 2 * DEPTHS,)),
        dma((ny,)),
        dma((ny,)),
        dma((2, PIECES * ny // 2)),
        dma((2, PIECES * ny // 2)),
        dma((2, 2 * ny)),
        dma((2, 2 * ny)),
        dma((3,)),
        dma((3,)),
        dma((2, 6)),
        dma((2, 6)),
        dma((2, ny)),
        dma((2, ny)),
        dma((2, NZ // ny)),
        dma((2, NZ)),
        dma((2, ny)),
        dma((2,)),
    ]
    hbm = pl.BlockSpec(memory_space=pl.ANY)
    in_vmem = pl.BlockSpec(memory_space=pltpu.VMEM)
    grad_w, query_grads, loss = pl.pallas_call(
        functools.partial(kernel, ny),
        out_shape=(
            jax.ShapeDtypeStruct((rows, width), F32),
            jax.ShapeDtypeStruct((lanes, width), F32),
            jax.ShapeDtypeStruct((1, users), F32),
        ),
        in_specs=[hbm, hbm, hbm, in_vmem, in_vmem, pl.BlockSpec(memory_space=pltpu.SMEM)],
        out_specs=(in_vmem, hbm, in_vmem),
        scratch_shapes=scratch,
        compiler_params=pltpu.CompilerParams(
            collective_id=0, has_side_effects=True, vmem_limit_bytes=53 * 1024 * 1024
        ),
    )(features, w_out, interests.reshape(lanes, width), neg_tiles.T, positives.reshape(1, users), tile_valid)
    return grad_w, query_grads.reshape(users, kk, width), loss.reshape(users)


def solution(mesh):
    in_specs = (
        P(("user", "item"), None),
        P(),
        P(("user", "item"), None, None),
        P(("user", "item"), None),
        P(("user", "item")),
        P(("user", "item")),
    )
    out_specs = (P("item", None), P(("user", "item"), None, None), P(("user", "item")))
    body = functools.partial(local, mesh.shape["user"])
    return jax.shard_map(body, mesh=mesh, in_specs=in_specs, out_specs=out_specs, check_vma=False)
```

time: 441 us -> 85 us (0.19)
  waiting for transfers between devices: 345 us -> 0 us
  Pallas kernels: 0 us -> 79.8 us
  blocking collectives: 48.8 us -> 0 us
  matrix products: 19 us -> 0 us
  between operations: 14.5 us -> 0.67 us
  other arithmetic: 6.18 us -> 0 us
    unnamed x4 -> x0, waiting for transfers between devices: 268 us -> none
    pallas_call x0 -> x1, Pallas kernels: none -> 79.8 us  [local(): pl.pallas_call(functools.partial(kernel, ny), out_shape=(jax.ShapeDtypeSt...]
    reduce_scatter x1 -> x0, waiting for transfers between devices: 45.6 us -> none  [local(): lax.psum_scatter(item_part, 'user', scatter_dimension=0, tiled=True)]
    all_gather x1 -> x0, waiting for transfers between devices: 32 us -> none  [local(): lax.all_gather(embedded, 'user', axis=0, tiled=True)]
    psum x1 -> x0, blocking collectives: 31.2 us -> none  [local(): grad_w = lax.psum(rows_part, 'user')]
    dot_general x5 -> x0, matrix products: 19 us -> none  [the longest x1 5.46 us: local(): lax.dot_general(flat_grad, queries, (((0,), (0,)), ((), ())), preferred_e...]
    unnamed x1 -> x0, blocking collectives: 17.6 us -> none
    reduce_sum x3 -> x0, other arithmetic: 4.56 us -> none  [the longest x1 3.22 us: local(): denominator = pos_term + jnp.sum(exp_terms, axis=-1)]
  transfers between devices with their start and end apart: 3 -> 0, of which waited for: 3 -> 0; matrix products, arithmetic and copies ran while one was open for 2% -> 0% of each run, Pallas kernels for 0% -> 0%
where the time goes in v1:
time: 85 us; the launch traced here: 84 us
  Pallas kernels  79.8 us (94%)
  local copies, waits for them, and re-layouts  3.53 us (4%)
    pallas_call x1, Pallas kernels, local(): pl.pallas_call(functools.partial(kernel, ny), out_shape=(jax.ShapeDtypeSt...  79.8 us
    unnamed x11, local copies, waits for them, and re-layouts  3.53 us

profile of v1, /device:TPU:6, one launch (start us, length us, event | category | flops | bytes accessed | tf_op | source)
XLA Modules:
  0.0 84.0 jit_solution(15871400526600353641)
XLA Ops:
  0.6 0.0 copy-start.1
  0.6 0.0 copy-start.2
  0.7 0.0 copy-start.3
  0.7 0.7 copy-done.1
  1.3 0.0 copy-done.2
  1.3 0.0 copy-done.3
  1.3 0.0 copy-start
  1.3 0.9 %copy-done = bf16[64,8,256]{2,1,0:T(8,128)(2,1)S(1)} copy-done((bf16[64,8,256]{2,1,0:T(8,128)(2,1)S(1)}, bf16[64,8,256]{2,1,0:T(8,128)(2,1)}, u32[]{:S(2)}) %copy-start) | copy-done | bytes 262168
  2.3 79.8 %shard_map.85 = (f32[16,256]{1,0:T(8,128)S(1)}, f32[512,256]{1,0:T(8,128)S(1)}, f32[1,64]{1,0:T(1,128)S(1)}) custom-call(bf16[256,2048]{1,0:T(8,128)(2,1)} %refs_0_.1, bf16[2048,256]{1,0:T(8,128)(2,1)} %refs_1_.1, bf16[512,256]{1,0:T(8,128)(2,1)S(1)} %bitcast.6, s32[4,64]{1,0:T(4,128)S(1)} %bitcast.7, s32[1,64]{1,0:T(1,128)S(1)} %bitcast.8, s32[2]{0:T(128)S(1)} %copy-done.3), custom_call_target="tpu_custom_call" | custom-call | tf_op jit(solution)/shard_map/pallas_call | solution.py:558
  82.1 0.6 copy.12
  82.7 0.8 copy.13
  83.5 0.5 copy.14
Async XLA Ops:
  0.6 0.7 copy-start.1
  0.6 0.7 copy-start.2
  0.7 0.7 copy-start.3
  1.3 1.0 %copy-start = (bf16[64,8,256]{2,1,0:T(8,128)(2,1)S(1)}, bf16[64,8,256]{2,1,0:T(8,128)(2,1)}, u32[]{:S(2)}) copy-start(bf16[64,8,256]{2,1,0:T(8,128)(2,1)} %param.8) | copy-start | bytes 786436

commit v2 on v1

--- a/solution.py
+++ b/solution.py
@@ -394,6 +394,7 @@
         x_send(h, 5, r.x_down.at[h, pl.ds(mid, mid)], r.xr_down.at[h, pl.ds(mid, mid)], False)
 
     per_y = NZ // ny
+    far_first = sorted(range(1, ny), key=lambda d: -min(d, ny - d))
 
     def y_stage(h):
         for kind in (2, 3, 4, 5):
@@ -401,12 +402,12 @@
         total = (r.x_own[h] + r.xr_up[h].astype(F32) + r.xr_down[h].astype(F32)).reshape(ny, per_y, 16, TILE)
         r.y_own[h] = total
         r.y_send[h] = total.astype(BF16)
-        y_copy[h] = [
-            send(
+        y_copy[h] = {
+            d: send(
                 r.y_send.at[h, lax.rem(y + d, ny)], r.y_recv.at[h, d], r.y_ssem.at[h, d], r.y_rsem.at[h, d], y_peer(d)
             )
-            for d in range(1, ny)
-        ]
+            for d in far_first
+        }
 
     def z_copy(h, i, sender):
         owner = y * per_y + i
@@ -421,8 +422,8 @@
 
     def z_stage(h):
         total = r.y_own[h, y]
-        for d, copy in enumerate(y_copy[h], 1):
-            copy.wait_recv()
+        for d in range(1, ny):
+            y_copy[h][d].wait_recv()
             total = total + r.y_recv[h, d].astype(F32)
         r.z_own[h] = total
         r.z_send[h] = total.astype(BF16)
@@ -453,7 +454,7 @@
                 return total + r.z_recv[h, sender].astype(F32)
 
             r.g_buf[h] = lax.fori_loop(1, NZ, add, r.z_own[h, lax.rem(z, per_y)])
-            for d in range(1, ny):
+            for d in far_first:
                 g_copy(h, d).start()
 
     def finish(h):

time: 85 us -> 85 us (level)
  no operation moved by 1% of the time
where the time goes in v2:
time: 85 us; the launch traced here: 83.7 us
  Pallas kernels  79.5 us (94%)
  local copies, waits for them, and re-layouts  3.53 us (4%)
    pallas_call x1, Pallas kernels, local(): pl.pallas_call(functools.partial(kernel, ny), out_shape=(jax.ShapeDtypeSt...  79.5 us
    unnamed x11, local copies, waits for them, and re-layouts  3.53 us

profile of v2, /device:TPU:6, one launch (start us, length us, event | category | flops | bytes accessed | tf_op | source)
XLA Modules:
  0.0 83.7 jit_solution(6612379165019868222)
XLA Ops:
  0.6 0.0 copy-start.1
  0.6 0.0 copy-start.2
  0.7 0.0 copy-start.3
  0.7 0.7 copy-done.1
  1.3 0.0 copy-done.2
  1.3 0.0 copy-done.3
  1.3 0.0 copy-start
  1.3 0.9 %copy-done = bf16[64,8,256]{2,1,0:T(8,128)(2,1)S(1)} copy-done((bf16[64,8,256]{2,1,0:T(8,128)(2,1)S(1)}, bf16[64,8,256]{2,1,0:T(8,128)(2,1)}, u32[]{:S(2)}) %copy-start) | copy-done | bytes 262168
  2.3 79.5 %shard_map.85 = (f32[16,256]{1,0:T(8,128)S(1)}, f32[512,256]{1,0:T(8,128)S(1)}, f32[1,64]{1,0:T(1,128)S(1)}) custom-call(bf16[256,2048]{1,0:T(8,128)(2,1)} %refs_0_.1, bf16[2048,256]{1,0:T(8,128)(2,1)} %refs_1_.1, bf16[512,256]{1,0:T(8,128)(2,1)S(1)} %bitcast.6, s32[4,64]{1,0:T(4,128)S(1)} %bitcast.7, s32[1,64]{1,0:T(1,128)S(1)} %bitcast.8, s32[2]{0:T(128)S(1)} %copy-done.3), custom_call_target="tpu_custom_call" | custom-call | tf_op jit(solution)/shard_map/pallas_call | solution.py:559
  81.8 0.6 copy.12
  82.4 0.8 copy.13
  83.2 0.5 copy.14
Async XLA Ops:
  0.6 0.7 copy-start.1
  0.6 0.7 copy-start.2
  0.7 0.7 copy-start.3
  1.3 1.0 %copy-start = (bf16[64,8,256]{2,1,0:T(8,128)(2,1)S(1)}, bf16[64,8,256]{2,1,0:T(8,128)(2,1)}, u32[]{:S(2)}) copy-start(bf16[64,8,256]{2,1,0:T(8,128)(2,1)} %param.8) | copy-start | bytes 786436
